TPU v7x, 32 devices: a whole 2x2x4 slice. The times are simulated.
32 devices in a mesh: pods: 2 (over y), inst: 4 (over z), tp: 4 (over x, core).
Axes of the slice: x: 2, y: 2, z: 4, core: 2. Of those that a mesh axis runs over, the one named last changes fastest.
Arguments:
- queries: bfloat16 [2048, 4096], P(('pods', 'inst'), 'tp'), parts along dimension 0, may hold values from -62 to 62
- cache_store: bfloat16 [2, 2048, 16, 512], P(None, ('pods', 'inst'), None, 'tp'), parts along dimension 1, may hold values from -6 to 6
- span_cache: bfloat16 [2, 2048, 512], P(None, ('pods', 'inst'), 'tp'), parts along dimension 1, may hold values from -6 to 6
- out_weight: bfloat16 [4096, 4096], P('tp'), may hold values from -0.5 to 0.5
- prefix_blocks: int32 [8], P(('pods', 'inst')), parts along dimension 0, may hold values from 1 to 512, 1280 in all
- span_lengths: int32 [8], P(('pods', 'inst')), parts along dimension 0, may hold values from 1 to 256, 768 in all
- hit_holders: int32 [8, 512, 1], P(('pods', 'inst')), parts along dimension 0, may hold values from 0 to 3; in each aligned block of 512 rows (0 to 511, 512 to 1023, ..., all dimensions but the last counted through in order) at most 160 rows name the same one
- hit_slots: int32 [8, 512], P(('pods', 'inst')), parts along dimension 0, may hold values from 0 to 255
- store_owners: int32 [8, 16, 1], P(('pods', 'inst')), parts along dimension 0, may hold values from 0 to 3; in each aligned block of 16 rows (0 to 15, 16 to 31, ..., all dimensions but the last counted through in order) at most 8 rows name the same one
Outputs:
- projected: bfloat16 [2048, 4096], P(('pods', 'inst', 'tp')), parts along dimension 0
- pushed_blocks: bfloat16 [2, 256, 16, 512], P(None, ('pods', 'inst'), None, 'tp'), parts along dimension 1
There are 2 independent parts, one for each index of `pods`. A program takes and returns all parts, laid end to end along the dimension named above; an argument that names none is the same for every part. Nothing has to cross between parts.
Inputs may be any that keep to these rules, and one draw needn't show every extreme that they name: `prefix_blocks`: the largest equals 512; they sum to 1280. `span_lengths`: the largest equals 256; they sum to 768. `hit_holders`: among the 512 entries of one instance no holder appears more than 160 times, and some instance names some holder exactly 160 times. Entries past the live prefix are present too. `store_owners`: among the 16 blocks of one instance no owner appears more than 8 times, and some instance names some owner exactly 8 times.
All inputs are finite; a program needn't handle non-finite values. No bound on the sum of `prefix_blocks` or of `span_lengths` on one device may be relied on, other than what follows from the above.
Results may differ from a plain program's by a relative error of at most 0.013.
Values may be sent and summed in bfloat16 or wider, within the bound.
No kernel may reach another device: no remote copies, remote signals or barrier semaphores. Data moves between devices by JAX's collectives and lax.ppermute only.
A program may use at most 128 MiB of HBM per device.

v0:
```python
import functools
import math

import jax
import jax.numpy as jnp
from jax import lax
from jax.experimental import pallas as pl
from jax.experimental.pallas import tpu as pltpu
from jax.sharding import PartitionSpec as P

LOW = -1e30
TOP = 2.0**100
TILE = 16
STACK = 4
VMEM_LIMIT = 32 * 1024 * 1024

SMEM = pl.BlockSpec(memory_space=pltpu.SMEM)
VMEM = pl.BlockSpec(memory_space=pltpu.VMEM)


def round_up(number, step):
    return -(-number // step) * step


def route_kernel(live_ref, holders_ref, slots_ref, q_ref, lists_ref, out_ref):
    peers, width = lists_ref.shape
    number = holders_ref.shape[1]
    padded = round_up(peers, 16)
    holder = lax.broadcasted_iota(jnp.int32, (padded, number), 0)
    entry = lax.broadcasted_iota(jnp.int32, (padded, number), 1)
    hot = (holders_ref[...] == holder) & (entry < live_ref[0])
    ones = jnp.where(hot, 1.0, 0.0)
    earlier = lax.broadcasted_iota(jnp.int32, (number, number), 0) < lax.broadcasted_iota(
        jnp.int32, (number, number), 1
    )
    ranks = jnp.dot(
        ones.astype(jnp.bfloat16),
        jnp.where(earlier, 1.0, 0.0).astype(jnp.bfloat16),
        preferred_element_type=jnp.float32,
    )
    rank = jnp.sum(ranks * ones, axis=0, keepdims=True)
    rank = jnp.broadcast_to(rank, (8, number)).T[:, :1].astype(jnp.int32)
    place = lax.broadcasted_iota(jnp.int32, (number, width), 1) == rank
    slots = jnp.where(hot, slots_ref[...], 0).astype(jnp.float32)
    lists = jnp.dot(
        slots.astype(jnp.bfloat16),
        jnp.where(place, 1.0, 0.0).astype(jnp.bfloat16),
        preferred_element_type=jnp.float32,
    )
    counts = jnp.sum(ones, axis=1, keepdims=True)
    last = lax.broadcasted_iota(jnp.int32, (padded, width), 1) == width - 1
    lists = jnp.where(last, counts, lists)[:peers]
    lists_ref[...] = lists.astype(jnp.int32)

    rows, columns = q_ref.shape
    out_ref[:rows, :] = q_ref[...]
    each = columns // width
    riders = out_ref.shape[0] - rows
    row = lax.broadcasted_iota(jnp.int32, (riders, columns), 0)
    tail = jnp.zeros((riders, columns), jnp.float32)
    for r in range(-(-peers // each)):
        line = [lists[h : h + 1] for h in range(r * each, min(peers, (r + 1) * each))]
        line += [jnp.zeros((1, width), jnp.float32)] * (each - len(line))
        tail = jnp.where(row == r, jnp.concatenate(line, axis=1), tail)
    out_ref[rows:, :] = tail.astype(jnp.bfloat16)


def route(live, holders, slots, queries, peers, width):
    rows, columns = queries.shape
    riders = round_up(-(-peers // (columns // width)), 16)
    return pl.pallas_call(
        route_kernel,
        out_shape=(
            jax.ShapeDtypeStruct((peers, width), jnp.int32),
            jax.ShapeDtypeStruct((rows + riders, columns), jnp.bfloat16),
        ),
        in_specs=[SMEM, VMEM, VMEM, VMEM],
        out_specs=(VMEM, VMEM),
        compiler_params=pltpu.CompilerParams(vmem_limit_bytes=VMEM_LIMIT),
        name="route",
    )(live, holders, slots, queries)


def score(q, keys):
    return lax.dot_general(q, keys, (((1,), (1,)), ((), ())), preferred_element_type=jnp.float32)


def twice(value):
    return jnp.concatenate([value, value], axis=1)


def attend(
    slot, count, store_ref, span_ref, span_live, q_ref, k_ref, v_ref, s_ref, ref_ref, acc_ref, rows,
    scale,
):
    block_rows, head_dim = store_ref.shape[2:]
    heads = q_ref.shape[0] // rows
    stack = rows * math.gcd(heads, STACK)
    stacks = q_ref.shape[0] // stack
    tiles = (count + TILE - 1) // TILE

    def fetch(tile, into):
        for j in range(TILE):
            index = tile * TILE + j
            here = slot(jnp.maximum(jnp.minimum(index, count - 1), 0))
            at = slice(j * block_rows, (j + 1) * block_rows)
            k_ref[into, at, :] = store_ref[0, here]
            block = store_ref[1, here]
            v_ref[into, at, :head_dim] = jnp.where(index < count, block, jnp.zeros_like(block))
            v_ref[into, at, head_dim:] = jnp.where(
                index < count, jnp.ones_like(block), jnp.zeros_like(block)
            )

    def start():
        if span_ref is None:
            acc_ref[...] = jnp.zeros_like(acc_ref)
            return
        keys = span_ref.shape[1]
        key = lax.broadcasted_iota(jnp.int32, (rows, keys), 1)
        row = lax.broadcasted_iota(jnp.int32, (rows, keys), 0)
        mask = (key <= row) & (key < span_live)
        values = jnp.concatenate(
            [span_ref[1], jnp.ones((keys, head_dim), jnp.bfloat16)], axis=1
        )
        s = score(q_ref[:rows, :], span_ref[0])
        for g in range(heads):
            at = slice(g * rows, (g + 1) * rows)
            if g + 1 < heads:
                following = score(q_ref[(g + 1) * rows : (g + 2) * rows, :], span_ref[0])
            s = jnp.where(mask, s, LOW)
            top = jnp.max(s, axis=1, keepdims=True)
            ref_ref[at, :] = jnp.broadcast_to(top, (rows, head_dim))
            p = jnp.exp2((s - top) * scale).astype(jnp.bfloat16)
            acc_ref[at, :] = jnp.dot(p, values, preferred_element_type=jnp.float32)
            s = following

    start()

    @pl.when(count > 0)
    def _():
        fetch(0, 0)
        if span_ref is None:
            few = score(q_ref[...], k_ref[0, : 8 * block_rows, :])
            ref_ref[...] = jnp.broadcast_to(
                jnp.max(few, axis=1, keepdims=True), ref_ref.shape
            )
        s_ref[...] = score(q_ref[:stack, :], k_ref[0])

        def step(tile, carry):
            now = lax.rem(tile, 2)
            later = 1 - now
            keys, values = k_ref[now], v_ref[now]
            s = s_ref[...]
            fetch(tile + 1, later)
            for c in range(stacks):
                at = slice(c * stack, (c + 1) * stack)
                if c + 1 < stacks:
                    following = score(q_ref[(c + 1) * stack : (c + 2) * stack, :], keys)
                else:
                    s_ref[...] = score(q_ref[:stack, :], k_ref[later])
                p = jnp.exp2((s - twice(ref_ref[at, :])) * scale).astype(jnp.bfloat16)
                acc_ref[at, :] += jnp.dot(p, values, preferred_element_type=jnp.float32)
                s = following
            return carry

        lax.fori_loop(0, tiles, step, 0)
        beyond = jnp.max(jnp.where(acc_ref[:, head_dim:] < TOP, 0.0, 1.0))

        @pl.when(beyond > 0.0)
        def _():
            start()
            if span_ref is None:
                ref_ref[...] = jnp.full_like(ref_ref, LOW)

            def careful(tile, carry):
                fetch(tile, 0)

                def head(g, inner):
                    at = pl.ds(pl.multiple_of(g * rows, rows), rows)
                    s = score(q_ref[at, :], k_ref[0])
                    old = ref_ref[at, :]
                    new = jnp.maximum(old, jnp.max(s, axis=1, keepdims=True))
                    p = jnp.exp2((s - twice(new)) * scale).astype(jnp.bfloat16)
                    update = jnp.dot(p, v_ref[0], preferred_element_type=jnp.float32)
                    acc_ref[at, :] = (
                        acc_ref[at, :] * twice(jnp.exp2((old - new) * scale)) + update
                    )
                    ref_ref[at, :] = new
                    return inner

                return lax.fori_loop(0, heads, head, carry)

            lax.fori_loop(0, tiles, careful, 0)


def stack_heads(queries_ref, q_ref, rows):
    head_dim = q_ref.shape[1]
    for g in range(q_ref.shape[0] // rows):
        q_ref[g * rows : (g + 1) * rows, :] = queries_ref[
            :rows, g * head_dim : (g + 1) * head_dim
        ]


def write_logs(out_ref, logs):
    heads, rows = logs.shape
    first = logs.astype(jnp.bfloat16).astype(jnp.float32)
    rest = logs - first
    second = rest.astype(jnp.bfloat16).astype(jnp.float32)
    third = rest - second
    spare = jnp.zeros((heads, out_ref.shape[1] - 3 * rows), jnp.float32)
    line = jnp.concatenate([first, second, third, spare], axis=1)
    padding = jnp.zeros((16 - heads, out_ref.shape[1]), jnp.float32)
    out_ref[rows:, :] = jnp.concatenate([line, padding], axis=0).astype(jnp.bfloat16)


def finish(out_ref, ref_ref, acc_ref, rows, scale):
    head_dim = ref_ref.shape[1]
    heads = ref_ref.shape[0] // rows
    lane = lax.broadcasted_iota(jnp.int32, (rows, head_dim), 1)
    logs = jnp.zeros((rows, head_dim), jnp.float32)
    for g in range(heads):
        at = slice(g * rows, (g + 1) * rows)
        total = acc_ref[at, head_dim:]
        out_ref[:rows, g * head_dim : (g + 1) * head_dim] = (
            acc_ref[at, :head_dim] / total
        ).astype(jnp.bfloat16)
        logs = jnp.where(lane == g, ref_ref[at, :] * scale + jnp.log2(total), logs)
    write_logs(out_ref, logs.T[:heads])


def own_kernel(
    scale, me_ref, span_live_ref, lists_ref, queries_ref, store_ref, span_ref, out_ref,
    q_ref, k_ref, v_ref, s_ref, ref_ref, acc_ref,
):
    me = me_ref[0]
    rows = queries_ref.shape[0]
    stack_heads(queries_ref, q_ref, rows)
    attend(
        lambda index: lists_ref[me, index], lists_ref[me, lists_ref.shape[1] - 1], store_ref,
        span_ref, span_live_ref[0], q_ref, k_ref, v_ref, s_ref, ref_ref, acc_ref, rows, scale,
    )
    finish(out_ref, ref_ref, acc_ref, rows, scale)


def guest_kernel(
    scale, width, rows, me_ref, a_ref, b_ref, store_ref, after_ref, out_a_ref, out_b_ref,
    wide_ref, list_ref, sem_ref, q_ref, k_ref, v_ref, s_ref, ref_ref, acc_ref,
):
    each = a_ref.shape[1] // width
    me = me_ref[0]
    lane = pl.multiple_of(lax.rem(me, each) * width, 128)
    for which, loaded_ref in enumerate((a_ref, b_ref)):
        riders = loaded_ref[rows:, pl.ds(lane, width)].astype(jnp.float32)
        row = lax.broadcasted_iota(jnp.int32, riders.shape, 0)
        mine = jnp.sum(jnp.where(row == me // each, riders, 0.0), axis=0, keepdims=True)
        wide_ref[which : which + 1, :] = mine.astype(jnp.int32)
    copy = pltpu.make_async_copy(wide_ref, list_ref, sem_ref)
    copy.start()
    stack_heads(a_ref, q_ref, rows)
    copy.wait()
    for which, (loaded_ref, out_ref) in enumerate(((a_ref, out_a_ref), (b_ref, out_b_ref))):
        count = list_ref[which, width - 1]

        @pl.when(count > 0)
        def _():
            if which:
                stack_heads(loaded_ref, q_ref, rows)
            attend(
                lambda index: list_ref[which, index], count, store_ref, None, None,
                q_ref, k_ref, v_ref, s_ref, ref_ref, acc_ref, rows, scale,
            )
            finish(out_ref, ref_ref, acc_ref, rows, scale)

        @pl.when(count == 0)
        def _():
            out_ref[...] = jnp.zeros_like(out_ref)
            write_logs(out_ref, jnp.full((q_ref.shape[0] // rows, rows), LOW, jnp.float32))


def attention_scratch(heads, rows, head_dim, block_rows):
    keys = TILE * block_rows
    return [
        pltpu.VMEM((heads * rows, head_dim), jnp.bfloat16),
        pltpu.VMEM((2, keys, head_dim), jnp.bfloat16),
        pltpu.VMEM((2, keys, 2 * head_dim), jnp.bfloat16),
        pltpu.VMEM((rows * math.gcd(heads, STACK), keys), jnp.float32),
        pltpu.VMEM((heads * rows, head_dim), jnp.float32),
        pltpu.VMEM((heads * rows, 2 * head_dim), jnp.float32),
    ]


def attention_cost(rows, keys, head_dim, heads):
    return pl.CostEstimate(
        flops=4 * rows * keys * head_dim * heads,
        bytes_accessed=4 * 1024 * 1024,
        transcendentals=rows * keys * heads,
    )


def project_kernel(peers, heads, me_ref, span_live_ref, *refs):
    parts = refs[: 2 * peers - 1]
    weight_ref, out_ref, held_ref, att_ref, sem_ref = refs[2 * peers - 1 :]
    rows, features = att_ref.shape
    chunks, _, width = held_ref.shape
    head_dim = features // heads
    copies = [
        pltpu.make_async_copy(
            weight_ref.at[:, pl.ds(i * width, width)], held_ref.at[i], sem_ref.at[i]
        )
        for i in range(chunks)
    ]
    for copy in copies:
        copy.start()

    me = me_ref[0]
    logs = []
    for index, part in enumerate(parts):
        pieces = part[rows:, :].astype(jnp.float32)[:heads]
        log = pieces[:, :rows] + pieces[:, rows : 2 * rows] + pieces[:, 2 * rows : 3 * rows]
        if index:
            away = (index + 1) // 2
            valid = me >= away if index % 2 else me + away < peers
            log = jnp.where(valid, log, LOW)
        logs.append(log)
    top = functools.reduce(jnp.maximum, logs)
    weights = [jnp.exp2(log - top) for log in logs]
    inverse = 1.0 / functools.reduce(jnp.add, weights)
    row = lax.broadcasted_iota(jnp.int32, (heads, rows), 1)
    inverse = jnp.where(row < span_live_ref[0], inverse, 0.0)
    weights = [(weight * inverse).T for weight in weights]
    for g in range(heads):
        at = slice(g * head_dim, (g + 1) * head_dim)
        total = jnp.zeros((rows, head_dim), jnp.float32)
        for part, weight in zip(parts, weights):
            total += part[:rows, at].astype(jnp.float32) * weight[:, g : g + 1]
        att_ref[:, at] = total.astype(jnp.bfloat16)

    for i in range(chunks):
        copies[i].wait()
        out_ref[:, i * width : (i + 1) * width] = jnp.dot(
            att_ref[...], held_ref[i], preferred_element_type=jnp.float32
        ).astype(jnp.bfloat16)


def project(me, span_live, parts, out_weight, peers, heads):
    features, outputs = out_weight.shape
    rows = parts[0].shape[0] - 16
    width = 512
    chunks = outputs // width
    return pl.pallas_call(
        functools.partial(project_kernel, peers, heads),
        out_shape=jax.ShapeDtypeStruct((rows, outputs), jnp.bfloat16),
        in_specs=[SMEM, SMEM]
        + [VMEM] * len(parts)
        + [pl.BlockSpec(memory_space=pl.ANY)],
        out_specs=VMEM,
        scratch_shapes=[
            pltpu.VMEM((chunks, features, width), jnp.bfloat16),
            pltpu.VMEM((rows, features), jnp.bfloat16),
            pltpu.SemaphoreType.DMA((chunks,)),
        ],
        compiler_params=pltpu.CompilerParams(vmem_limit_bytes=VMEM_LIMIT),
        cost_estimate=pl.CostEstimate(
            flops=2 * rows * features * outputs,
            bytes_accessed=2 * (features + rows) * outputs,
            transcendentals=0,
        ),
        name="project",
    )(me, span_live, *parts, out_weight)


def pack_kernel(span_live_ref, owners_ref, span_ref, out_ref, counts_ref):
    peers = out_ref.shape[1]
    block_rows, head_dim = out_ref.shape[3:]
    out_ref[...] = jnp.zeros_like(out_ref)
    for k in range(peers):
        counts_ref[k] = 0
    row = lax.broadcasted_iota(jnp.int32, (block_rows, head_dim), 0)
    for b in range(span_ref.shape[1] // block_rows):
        owner = owners_ref[b]
        rank = counts_ref[owner]
        counts_ref[owner] = rank + 1
        keep = row + b * block_rows < span_live_ref[0]
        for side in range(2):
            block = span_ref[side, b * block_rows : (b + 1) * block_rows, :]
            out_ref[side, owner, rank] = jnp.where(keep, block, jnp.zeros_like(block))


def shards(
    queries,
    cache_store,
    span_cache,
    out_weight,
    prefix_blocks,
    span_lengths,
    hit_holders,
    hit_slots,
    store_owners,
):
    peers = lax.axis_size("inst")
    block_rows, head_dim = cache_store.shape[2:]
    rows, columns = queries.shape
    heads = columns // head_dim
    block_max = hit_slots.shape[1]
    cap = max(2, block_max * 5 // (4 * peers))
    new_count = rows // block_rows
    push_cap = max(2, 2 * new_count // peers)
    scale = math.log2(math.e) / math.sqrt(head_dim)
    me = lax.axis_index("inst").reshape(1)
    width = round_up(cap + 1, 128)
    part_shape = jax.ShapeDtypeStruct((rows + 16, columns), jnp.bfloat16)
    scratch = attention_scratch(heads, rows, head_dim, block_rows)
    params = pltpu.CompilerParams(vmem_limit_bytes=VMEM_LIMIT)

    def shift(value, by):
        pairs = [(i, i + by) for i in range(peers) if 0 <= i + by < peers]
        return lax.ppermute(value, "inst", pairs)

    lists, loaded = route(
        prefix_blocks, hit_holders.reshape(1, -1), hit_slots, queries, peers, width
    )
    from_left, from_right = shift(loaded, 1), shift(loaded, -1)
    own = pl.pallas_call(
        functools.partial(own_kernel, scale),
        out_shape=part_shape,
        in_specs=[SMEM, SMEM, SMEM, VMEM, VMEM, VMEM],
        out_specs=VMEM,
        scratch_shapes=scratch,
        compiler_params=params,
        cost_estimate=attention_cost(rows, 8 * rows, head_dim, heads),
        name="own_attention",
    )(me, span_lengths, lists, queries, cache_store, span_cache)

    parts, after = [own], own
    for away in range(1, peers):
        guests = (from_left, from_right)
        if away + 1 < peers:
            from_left, from_right, after = lax.optimization_barrier((*guests, after))
            from_left, from_right = shift(from_left, 1), shift(from_right, -1)
        part_a, part_b = pl.pallas_call(
            functools.partial(guest_kernel, scale, width, rows),
            out_shape=(part_shape, part_shape),
            in_specs=[SMEM, VMEM, VMEM, VMEM, pl.BlockSpec(memory_space=pl.ANY)],
            out_specs=(VMEM, VMEM),
            scratch_shapes=[
                pltpu.VMEM((2, width), jnp.int32),
                pltpu.SMEM((2, width), jnp.int32),
                pltpu.SemaphoreType.DMA,
                *scratch,
            ],
            compiler_params=params,
            cost_estimate=attention_cost(rows, 8 * rows, head_dim, heads),
            name="guest_attention",
        )(me, *guests, cache_store, after)
        after = part_a
        parts.append(shift(part_b, away))
        parts.append(shift(part_a, -away))

    partial = project(me, span_lengths, parts, out_weight, peers, heads)
    projected = lax.psum_scatter(partial, "tp", scatter_dimension=0, tiled=True)

    outgoing = pl.pallas_call(
        pack_kernel,
        out_shape=jax.ShapeDtypeStruct(
            (2, peers, push_cap, block_rows, head_dim), jnp.bfloat16
        ),
        in_specs=[SMEM, SMEM, VMEM],
        out_specs=VMEM,
        scratch_shapes=[pltpu.SMEM((peers,), jnp.int32)],
        compiler_params=pltpu.CompilerParams(vmem_limit_bytes=VMEM_LIMIT),
        name="pack_blocks",
    )(span_lengths, store_owners.reshape(-1), span_cache)
    incoming = lax.all_to_all(outgoing, "inst", split_axis=1, concat_axis=1, tiled=True)
    pushed_blocks = incoming.reshape(2, peers * push_cap, block_rows, head_dim)
    return (projected, pushed_blocks)


def solution(mesh):
    return jax.shard_map(
        shards,
        mesh=mesh,
        in_specs=(
            P(("pods", "inst"), "tp"),
            P(None, ("pods", "inst"), None, "tp"),
            P(None, ("pods", "inst"), "tp"),
            P("tp", None),
            P(("pods", "inst")),
            P(("pods", "inst")),
            P(("pods", "inst"), None, None),
            P(("pods", "inst"), None),
            P(("pods", "inst"), None, None),
        ),
        out_specs=(P(("pods", "inst", "tp"), None), P(None, ("pods", "inst"), None, "tp")),
        check_vma=False,
    )
```

profile of v0, /device:TPU:4, one launch (start us, length us, event | category | flops | bytes accessed | tf_op | source)
XLA Modules:
  0.0 273.0 jit_solution(17679102189035082020)
XLA Ops:
  7.2 0.0 reduce-scatter.2.cloned.1.call-start
  7.9 0.0 copy-start
  7.9 1.0 copy-done
  8.9 0.7 copy-done.4
  9.6 0.7 copy-done.5
  10.3 0.7 route.1
  11.0 3.5 %collective-permute-start = (bf16[272,1024]{1,0:T(8,128)(2,1)S(1)}, bf16[272,1024]{1,0:T(8,128)(2,1)S(1)}, u32[]{:S(2)}, u32[]{:S(2)}) collective-permute-start(bf16[272,1024]{1,0:T(8,128)(2,1)S(1)} %get-tuple-element.17), channel_id=1, source_target_pairs={{0,4},{4,8},{8,12},{1,5},{5,9},{9,13},{2,6},{6,10},{10,14},{3,7},{... | collective-permute-start | bytes 1671176 | tf_op jit(solution)/shard_map/ppermute | solution.py:417
  14.5 1.3 collective-permute-start.1
  16.4 0.0 copy-start.1
  16.4 1.0 copy-done.1
  17.5 0.9 copy-done.2
  18.4 1.6 copy-done.7
  20.0 45.3 %own_attention.1.after_ref.refs_0_ = bf16[272,1024]{1,0:T(8,128)(2,1)S(1)} custom-call(s32[1]{0:T(128)} %bitcast.me_ref, s32[1]{0:T(128)S(6)} %copy.15.span_live_ref, s32[4,256]{1,0:T(4,128)S(1)} %get-tuple-element.16.lists_ref, bf16[256,1024]{1,0:T(8,128)(2,1)S(1)} %copy-done.1, bf16[2,256,16,128]{3,2,1,0:T(8,128)(2,1)S(1)} %copy-done.7, ...), custom_call_target="tpu_custom_call" | custom-call | flops 2147483648 | bytes 4194304 | tf_op jit(solution)/shard_map/own_attention/pallas_call | solution.py:423
  65.3 0.0 copy-start.8
  65.3 0.0 collective-permute-done.a_ref
  65.3 0.0 collective-permute-done.1.b_ref
  65.3 1.5 collective-permute-start.4
  66.7 1.3 collective-permute-start.5
  68.0 19.0 %guest_attention.3 = (bf16[272,1024]{1,0:T(8,128)(2,1)S(1)}, bf16[272,1024]{1,0:T(8,128)(2,1)S(1)}) custom-call(s32[1]{0:T(128)} %bitcast.me_ref, bf16[272,1024]{1,0:T(8,128)(2,1)S(1)} %collective-permute-done.a_ref, bf16[272,1024]{1,0:T(8,128)(2,1)S(1)} %collective-permute-done.1.b_ref, bf16[2,256,16,128]{3,2,1,0:T(8,128)(2,1)S(1)} %copy-done.7, ...), custom_call_target="tpu_custom_call" | custom-call | flops 2147483648 | bytes 4194304 | tf_op jit(solution)/shard_map/guest_attention/pallas_call | solution.py:440
  87.0 0.0 collective-permute-done.4.a_ref
  87.0 0.0 collective-permute-done.5.b_ref
  87.0 35.3 %collective-permute-start.8 = (bf16[272,1024]{1,0:T(8,128)(2,1)S(1)}, bf16[272,1024]{1,0:T(8,128)(2,1)S(1)}, u32[]{:S(2)}, u32[]{:S(2)}) collective-permute-start(bf16[272,1024]{1,0:T(8,128)(2,1)S(1)} %collective-permute-done.4.a_ref), channel_id=1, source_target_pairs={{0,4},{4,8},{8,12},{1,5},{5,9},{9,13},{2,6},{6,10},{10,14},{3,7},{... | collective-permute-start | bytes 1671176 | tf_op jit(solution)/shard_map/ppermute | solution.py:417
  122.3 1.3 collective-permute-start.9
  123.6 1.3 collective-permute-start.3
  124.9 5.2 %collective-permute-start.2 = (bf16[272,1024]{1,0:T(8,128)(2,1)S(1)}, bf16[272,1024]{1,0:T(8,128)(2,1)S(1)}, u32[]{:S(2)}, u32[]{:S(2)}) collective-permute-start(bf16[272,1024]{1,0:T(8,128)(2,1)S(1)} %get-tuple-element.19), channel_id=1, source_target_pairs={{0,4},{4,8},{8,12},{1,5},{5,9},{9,13},{2,6},{6,10},{10,14},{3,7},{... | collective-permute-start | bytes 1671176 | tf_op jit(solution)/shard_map/ppermute | solution.py:417
  130.2 0.0 slice-start
  130.2 15.0 %guest_attention.4 = (bf16[272,1024]{1,0:T(8,128)(2,1)S(1)}, bf16[272,1024]{1,0:T(8,128)(2,1)S(1)}) custom-call(s32[1]{0:T(128)} %bitcast.me_ref, bf16[272,1024]{1,0:T(8,128)(2,1)S(1)} %collective-permute-done.4.a_ref, bf16[272,1024]{1,0:T(8,128)(2,1)S(1)} %collective-permute-done.5.b_ref, bf16[2,256,16,128]{3,2,1,0:T(8,128)(2,1)S(1)} %copy-done.8, ...), custom_call_target="tpu_custom_call" | custom-call | flops 2147483648 | bytes 4194304 | tf_op jit(solution)/shard_map/guest_attention/pallas_call | solution.py:440
  145.1 11.7 %collective-permute-start.6 = (bf16[272,1024]{1,0:T(8,128)(2,1)S(1)}, bf16[272,1024]{1,0:T(8,128)(2,1)S(1)}, u32[]{:S(2)}, u32[]{:S(2)}) collective-permute-start(bf16[272,1024]{1,0:T(8,128)(2,1)S(1)} %get-tuple-element.24), channel_id=1, source_target_pairs={{0,8},{4,12},{1,9},{5,13},{2,10},{6,14},{3,11},{7,15},{16,24},{20,... | collective-permute-start | bytes 1671176 | tf_op jit(solution)/shard_map/ppermute | solution.py:417
  156.8 0.0 collective-permute-done.8.a_ref
  156.9 0.0 slice-start.1
  156.9 1.6 collective-permute-start.7
  158.4 44.1 %guest_attention.5 = (bf16[272,1024]{1,0:T(8,128)(2,1)S(1)}, bf16[272,1024]{1,0:T(8,128)(2,1)S(1)}) custom-call(s32[1]{0:T(128)} %bitcast.me_ref, bf16[272,1024]{1,0:T(8,128)(2,1)S(1)} %collective-permute-done.8.a_ref, bf16[272,1024]{1,0:T(8,128)(2,1)S(1)} %collective-permute-done.9.b_ref, bf16[2,256,16,128]{3,2,1,0:T(8,128)(2,1)S(1)} %copy-done.8, ...), custom_call_target="tpu_custom_call" | custom-call | flops 2147483648 | bytes 4194304 | tf_op jit(solution)/shard_map/guest_attention/pallas_call | solution.py:440
  202.5 9.0 %collective-permute-start.10 = (bf16[272,1024]{1,0:T(8,128)(2,1)S(1)}, bf16[272,1024]{1,0:T(8,128)(2,1)S(1)}, u32[]{:S(2)}, u32[]{:S(2)}) collective-permute-start(bf16[272,1024]{1,0:T(8,128)(2,1)S(1)} %get-tuple-element.28), channel_id=1, source_target_pairs={{0,12},{1,13},{2,14},{3,15},{16,28},{17,29},{18,30},{19,31}} | collective-permute-start | bytes 1671176 | tf_op jit(solution)/shard_map/ppermute | solution.py:417
  211.6 0.0 collective-permute-done.3.refs_2_
  211.6 1.5 collective-permute-start.11
  213.1 0.0 collective-permute-done.2.refs_1_
  213.1 0.0 collective-permute-done.6.refs_3_
  213.1 8.3 %collective-permute-done.10.refs_5_ = bf16[272,1024]{1,0:T(8,128)(2,1)S(1)} collective-permute-done((bf16[272,1024]{1,0:T(8,128)(2,1)S(1)}, bf16[272,1024]{1,0:T(8,128)(2,1)S(1)}, u32[]{:S(2)}, u32[]{:S(2)}) %collective-permute-start.10) | collective-permute-done | bytes 557088 | tf_op jit(solution)/shard_map/ppermute | solution.py:417
  221.5 6.0 %collective-permute-done.11.refs_6_ = bf16[272,1024]{1,0:T(8,128)(2,1)S(1)} collective-permute-done((bf16[272,1024]{1,0:T(8,128)(2,1)S(1)}, bf16[272,1024]{1,0:T(8,128)(2,1)S(1)}, u32[]{:S(2)}, u32[]{:S(2)}) %collective-permute-start.11) | collective-permute-done | bytes 557088 | tf_op jit(solution)/shard_map/ppermute | solution.py:417
  227.4 9.0 %project.1 = bf16[256,4096]{1,0:T(8,128)(2,1)} custom-call(s32[1]{0:T(128)} %bitcast.me_ref, s32[1]{0:T(128)S(6)} %copy.15.span_live_ref, bf16[272,1024]{1,0:T(8,128)(2,1)S(1)} %own_attention.1.after_ref.refs_0_, bf16[272,1024]{1,0:T(8,128)(2,1)S(1)} %collective-permute-done.2.refs_1_, bf16[272,1024]{1,0:T(8,128)(2,1)S(1)} %collective-permute-done.3.refs_2_, ...), custom_call_target="tpu_custom_call" | custom-call | flops 2147483648 | bytes 10485760 | tf_op jit(solution)/shard_map/project/pallas_call | solution.py:350
  236.4 0.0 copy-start.3
  236.4 0.0 copy-start.6
  236.4 0.0 reduce-scatter.2.cloned.1.call-update
  236.4 0.9 copy-done.3
  237.3 0.6 pack_blocks.1
  238.0 9.5 %all_to_all.5 = bf16[2,4,8,16,128]{4,3,2,0,1:T(8,128)(2,1)S(1)} all-to-all(bf16[2,4,8,16,128]{4,3,2,0,1:T(8,128)(2,1)S(1)} %copy.12), channel_id=1, replica_groups=mesh['pods'=2,'inst'=4,'tp'=4] {'inst'}, dimensions={1} | all-to-all | bytes 524288 | tf_op jit(solution)/shard_map/all_to_all | solution.py:473
  247.5 0.7 copy.13
  248.2 18.0 %reduce-scatter.2.cloned.1.call-done = bf16[64,4096]{1,0:T(8,128)(2,1)} async-done(((bf16[256,4096]{1,0:T(8,128)(2,1)}), bf16[64,4096]{1,0:T(8,128)(2,1)}) %reduce-scatter.2.cloned.1.call-update) | async-done | bytes 524304 | tf_op jit(solution)/shard_map/reduce_scatter | solution.py:460
  (12 shorter events, 0.0 us)
Async XLA Ops:
  7.2 259.0 %reduce-scatter.2.cloned.1.call-start = ((), (), s32[]{:S(2)}) async-start(), calls=%async_computation.2 | async-start | bytes 2621440 | tf_op jit(solution)/shard_map/reduce_scatter | solution.py:460
  7.9 1.0 copy-start
  8.9 0.7 copy-start.4
  9.6 0.7 copy-start.5
  11.0 54.3 %collective-permute-start = (bf16[272,1024]{1,0:T(8,128)(2,1)S(1)}, bf16[272,1024]{1,0:T(8,128)(2,1)S(1)}, u32[]{:S(2)}, u32[]{:S(2)}) collective-permute-start(bf16[272,1024]{1,0:T(8,128)(2,1)S(1)} %get-tuple-element.17), channel_id=1, source_target_pairs={{0,4},{4,8},{8,12},{1,5},{5,9},{9,13},{2,6},{6,10},{10,14},{3,7},{... | collective-permute-start | bytes 1671176 | tf_op jit(solution)/shard_map/ppermute | solution.py:417
  14.5 50.8 %collective-permute-start.1 = (bf16[272,1024]{1,0:T(8,128)(2,1)S(1)}, bf16[272,1024]{1,0:T(8,128)(2,1)S(1)}, u32[]{:S(2)}, u32[]{:S(2)}) collective-permute-start(bf16[272,1024]{1,0:T(8,128)(2,1)S(1)} %get-tuple-element.17), channel_id=1, source_target_pairs={{4,0},{8,4},{12,8},{5,1},{9,5},{13,9},{6,2},{10,6},{14,10},{7,3},{... | collective-permute-start | bytes 1671176 | tf_op jit(solution)/shard_map/ppermute | solution.py:417
  16.4 1.0 copy-start.1
  17.5 0.9 copy-start.2
  18.4 1.6 copy-start.7
  65.3 64.9 %copy-start.8 = (bf16[2,256,16,128]{3,2,1,0:T(8,128)(2,1)S(1)}, bf16[2,256,16,128]{3,2,1,0:T(8,128)(2,1)}, u32[]{:S(2)}) copy-start(bf16[2,256,16,128]{3,2,1,0:T(8,128)(2,1)} %store_ref.7) | copy-start | bytes 6291460
  65.3 21.7 %collective-permute-start.4 = (bf16[272,1024]{1,0:T(8,128)(2,1)S(1)}, bf16[272,1024]{1,0:T(8,128)(2,1)S(1)}, u32[]{:S(2)}, u32[]{:S(2)}) collective-permute-start(bf16[272,1024]{1,0:T(8,128)(2,1)S(1)} %collective-permute-done.a_ref), channel_id=1, source_target_pairs={{0,4},{4,8},{8,12},{1,5},{5,9},{9,13},{2,6},{6,10},{10,14},{3,7},{... | collective-permute-start | bytes 1671176 | tf_op jit(solution)/shard_map/ppermute | solution.py:417
  66.7 20.3 %collective-permute-start.5 = (bf16[272,1024]{1,0:T(8,128)(2,1)S(1)}, bf16[272,1024]{1,0:T(8,128)(2,1)S(1)}, u32[]{:S(2)}, u32[]{:S(2)}) collective-permute-start(bf16[272,1024]{1,0:T(8,128)(2,1)S(1)} %collective-permute-done.1.b_ref), channel_id=1, source_target_pairs={{4,0},{8,4},{12,8},{5,1},{9,5},{13,9},{6,2},{10,6},{14,10},{7,3},{... | collective-permute-start | bytes 1671176 | tf_op jit(solution)/shard_map/ppermute | solution.py:417
  87.0 69.8 %collective-permute-start.8 = (bf16[272,1024]{1,0:T(8,128)(2,1)S(1)}, bf16[272,1024]{1,0:T(8,128)(2,1)S(1)}, u32[]{:S(2)}, u32[]{:S(2)}) collective-permute-start(bf16[272,1024]{1,0:T(8,128)(2,1)S(1)} %collective-permute-done.4.a_ref), channel_id=1, source_target_pairs={{0,4},{4,8},{8,12},{1,5},{5,9},{9,13},{2,6},{6,10},{10,14},{3,7},{... | collective-permute-start | bytes 1671176 | tf_op jit(solution)/shard_map/ppermute | solution.py:417
  122.3 36.1 %collective-permute-start.9 = (bf16[272,1024]{1,0:T(8,128)(2,1)S(1)}, bf16[272,1024]{1,0:T(8,128)(2,1)S(1)}, u32[]{:S(2)}, u32[]{:S(2)}) collective-permute-start(bf16[272,1024]{1,0:T(8,128)(2,1)S(1)} %collective-permute-done.5.b_ref), channel_id=1, source_target_pairs={{4,0},{8,4},{12,8},{5,1},{9,5},{13,9},{6,2},{10,6},{14,10},{7,3},{... | collective-permute-start | bytes 1671176 | tf_op jit(solution)/shard_map/ppermute | solution.py:417
  123.6 87.9 %collective-permute-start.3 = (bf16[272,1024]{1,0:T(8,128)(2,1)S(1)}, bf16[272,1024]{1,0:T(8,128)(2,1)S(1)}, u32[]{:S(2)}, u32[]{:S(2)}) collective-permute-start(bf16[272,1024]{1,0:T(8,128)(2,1)S(1)} %get-tuple-element.23.after_ref), channel_id=1, source_target_pairs={{4,0},{8,4},{12,8},{5,1},{9,5},{13,9},{6,2},{10,6},{14,10},{7,3},{... | collective-permute-start | bytes 1671176 | tf_op jit(solution)/shard_map/ppermute | solution.py:417
  124.9 88.2 %collective-permute-start.2 = (bf16[272,1024]{1,0:T(8,128)(2,1)S(1)}, bf16[272,1024]{1,0:T(8,128)(2,1)S(1)}, u32[]{:S(2)}, u32[]{:S(2)}) collective-permute-start(bf16[272,1024]{1,0:T(8,128)(2,1)S(1)} %get-tuple-element.19), channel_id=1, source_target_pairs={{0,4},{4,8},{8,12},{1,5},{5,9},{9,13},{2,6},{6,10},{10,14},{3,7},{... | collective-permute-start | bytes 1671176 | tf_op jit(solution)/shard_map/ppermute | solution.py:417
  130.2 97.2 %slice-start = ((s8[8388608]{0:T(1024)(128)(4,1)}), s8[4194304]{0:T(1024)(128)(4,1)S(1)}, s32[]{:S(2)}) async-start(s8[8388608]{0:T(1024)(128)(4,1)} %bitcast.4), calls=%async_computation.3 | async-start | bytes 8388608
  145.1 68.0 %collective-permute-start.6 = (bf16[272,1024]{1,0:T(8,128)(2,1)S(1)}, bf16[272,1024]{1,0:T(8,128)(2,1)S(1)}, u32[]{:S(2)}, u32[]{:S(2)}) collective-permute-start(bf16[272,1024]{1,0:T(8,128)(2,1)S(1)} %get-tuple-element.24), channel_id=1, source_target_pairs={{0,8},{4,12},{1,9},{5,13},{2,10},{6,14},{3,11},{7,15},{16,24},{20,... | collective-permute-start | bytes 1671176 | tf_op jit(solution)/shard_map/ppermute | solution.py:417
  156.9 70.6 %slice-start.1 = ((s8[8388608]{0:T(1024)(128)(4,1)}), s8[4194304]{0:T(1024)(128)(4,1)S(1)}, s32[]{:S(2)}) async-start(s8[8388608]{0:T(1024)(128)(4,1)} %bitcast.4), calls=%async_computation.4 | async-start | bytes 8388608
  156.9 56.3 %collective-permute-start.7 = (bf16[272,1024]{1,0:T(8,128)(2,1)S(1)}, bf16[272,1024]{1,0:T(8,128)(2,1)S(1)}, u32[]{:S(2)}, u32[]{:S(2)}) collective-permute-start(bf16[272,1024]{1,0:T(8,128)(2,1)S(1)} %get-tuple-element.25.after_ref), channel_id=1, source_target_pairs={{8,0},{12,4},{9,1},{13,5},{10,2},{14,6},{11,3},{15,7},{24,16},{28,... | collective-permute-start | bytes 1671176 | tf_op jit(solution)/shard_map/ppermute | solution.py:417
  202.5 18.9 %collective-permute-start.10 = (bf16[272,1024]{1,0:T(8,128)(2,1)S(1)}, bf16[272,1024]{1,0:T(8,128)(2,1)S(1)}, u32[]{:S(2)}, u32[]{:S(2)}) collective-permute-start(bf16[272,1024]{1,0:T(8,128)(2,1)S(1)} %get-tuple-element.28), channel_id=1, source_target_pairs={{0,12},{1,13},{2,14},{3,15},{16,28},{17,29},{18,30},{19,31}} | collective-permute-start | bytes 1671176 | tf_op jit(solution)/shard_map/ppermute | solution.py:417
  211.6 15.8 %collective-permute-start.11 = (bf16[272,1024]{1,0:T(8,128)(2,1)S(1)}, bf16[272,1024]{1,0:T(8,128)(2,1)S(1)}, u32[]{:S(2)}, u32[]{:S(2)}) collective-permute-start(bf16[272,1024]{1,0:T(8,128)(2,1)S(1)} %get-tuple-element.29), channel_id=1, source_target_pairs={{12,0},{13,1},{14,2},{15,3},{28,16},{29,17},{30,18},{31,19}} | collective-permute-start | bytes 1671176 | tf_op jit(solution)/shard_map/ppermute | solution.py:417
  236.4 0.9 copy-start.3
  236.4 0.9 copy-start.6
Sparse Core Ops, SparseCore 0:
  236.6 29.5 reduce-scatter.1
where the time goes:
time: 278 us; the launch traced here: 273 us
  Pallas kernels  134 us (48%)
  starting transfers between devices  74.5 us (27%)
  waiting for transfers between devices  32.3 us (12%)
  between operations  15.6 us (6%)
  blocking collectives  9.51 us (3%)
  local copies, waits for them, and re-layouts  7.56 us (3%)
    pallas_call x3, Pallas kernels, shards(): pl.pallas_call(functools.partial(guest_kernel, scale, width, rows), out_s...  78 us
    ppermute x12, starting transfers between devices, shift(): return lax.ppermute(value, 'inst', pairs)  74.4 us
    pallas_call x1, Pallas kernels, shards(): pl.pallas_call(functools.partial(own_kernel, scale), out_shape=part_shape...  45.3 us
    reduce_scatter x1, waiting for transfers between devices, shards(): projected = lax.psum_scatter(partial, 'tp', scatter_dimension=0, tiled=True)  18 us
    ppermute x12, waiting for transfers between devices, shift(): return lax.ppermute(value, 'inst', pairs)  14.3 us
    all_to_all x1, blocking collectives, shards(): lax.all_to_all(outgoing, 'inst', split_axis=1, concat_axis=1, tiled=True)  9.51 us
    pallas_call x1, Pallas kernels, project(): pl.pallas_call(functools.partial(project_kernel, peers, heads), out_shape...  8.97 us
    unnamed x22, local copies, waits for them, and re-layouts  6.82 us
  transfers between devices with their start and end apart: 13, of which 3 were waited for; matrix products, arithmetic and copies ran while one was open for 0% of the time, Pallas kernels for 45%

commit v1 on v0

--- a/solution.py
+++ b/solution.py
@@ -16,13 +16,27 @@
 
 SMEM = pl.BlockSpec(memory_space=pltpu.SMEM)
 VMEM = pl.BlockSpec(memory_space=pltpu.VMEM)
+HBM = pl.BlockSpec(memory_space=pltpu.HBM)
 
 
 def round_up(number, step):
     return -(-number // step) * step
 
 
-def route_kernel(live_ref, holders_ref, slots_ref, q_ref, lists_ref, out_ref):
+def route_kernel(
+    live_ref, holders_in, slots_in, q_in, lists_ref, out_ref, holders_ref, slots_ref, tail_ref, sems
+):
+    rows, columns = q_in.shape
+    loading = [
+        pltpu.make_async_copy(holders_in, holders_ref, sems.at[0]),
+        pltpu.make_async_copy(slots_in, slots_ref, sems.at[1]),
+    ]
+    passing = pltpu.make_async_copy(q_in, out_ref.at[pl.ds(0, rows)], sems.at[2])
+    for copy in loading:
+        copy.start()
+    passing.start()
+    for copy in loading:
+        copy.wait()
     peers, width = lists_ref.shape
     number = holders_ref.shape[1]
     padded = round_up(peers, 16)
@@ -52,17 +66,19 @@
     lists = jnp.where(last, counts, lists)[:peers]
     lists_ref[...] = lists.astype(jnp.int32)
 
-    rows, columns = q_ref.shape
-    out_ref[:rows, :] = q_ref[...]
     each = columns // width
-    riders = out_ref.shape[0] - rows
+    riders = tail_ref.shape[0]
     row = lax.broadcasted_iota(jnp.int32, (riders, columns), 0)
     tail = jnp.zeros((riders, columns), jnp.float32)
     for r in range(-(-peers // each)):
         line = [lists[h : h + 1] for h in range(r * each, min(peers, (r + 1) * each))]
         line += [jnp.zeros((1, width), jnp.float32)] * (each - len(line))
         tail = jnp.where(row == r, jnp.concatenate(line, axis=1), tail)
-    out_ref[rows:, :] = tail.astype(jnp.bfloat16)
+    tail_ref[...] = tail.astype(jnp.bfloat16)
+    riding = pltpu.make_async_copy(tail_ref, out_ref.at[pl.ds(rows, riders)], sems.at[3])
+    riding.start()
+    passing.wait()
+    riding.wait()
 
 
 def route(live, holders, slots, queries, peers, width):
@@ -74,9 +90,15 @@
             jax.ShapeDtypeStruct((peers, width), jnp.int32),
             jax.ShapeDtypeStruct((rows + riders, columns), jnp.bfloat16),
         ),
-        in_specs=[SMEM, VMEM, VMEM, VMEM],
-        out_specs=(VMEM, VMEM),
-        compiler_params=pltpu.CompilerParams(vmem_limit_bytes=VMEM_LIMIT),
+        in_specs=[SMEM, HBM, HBM, HBM],
+        out_specs=(VMEM, HBM),
+        scratch_shapes=[
+            pltpu.VMEM(holders.shape, jnp.int32),
+            pltpu.VMEM(slots.shape, jnp.int32),
+            pltpu.VMEM((riders, columns), jnp.bfloat16),
+            pltpu.SemaphoreType.DMA((4,)),
+        ],
+        compiler_params=pltpu.CompilerParams(vmem_limit_bytes=62 * 1024 * 1024),
         name="route",
     )(live, holders, slots, queries)
 
@@ -91,7 +113,7 @@
 
 def attend(
     slot, count, store_ref, span_ref, span_live, q_ref, k_ref, v_ref, s_ref, ref_ref, acc_ref, rows,
-    scale,
+    scale, stored=None,
 ):
     block_rows, head_dim = store_ref.shape[2:]
     heads = q_ref.shape[0] // rows
@@ -135,6 +157,8 @@
             s = following
 
     start()
+    if stored is not None:
+        stored()
 
     @pl.when(count > 0)
     def _():
@@ -229,15 +253,26 @@
 
 
 def own_kernel(
-    scale, me_ref, span_live_ref, lists_ref, queries_ref, store_ref, span_ref, out_ref,
-    q_ref, k_ref, v_ref, s_ref, ref_ref, acc_ref,
+    scale, me_ref, span_live_ref, lists_ref, queries_in, store_in, span_in, out_ref,
+    queries_ref, store_ref, span_ref, sems, q_ref, k_ref, v_ref, s_ref, ref_ref, acc_ref,
 ):
     me = me_ref[0]
     rows = queries_ref.shape[0]
+    copies = [
+        pltpu.make_async_copy(source, target, sems.at[i])
+        for i, (source, target) in enumerate(
+            ((queries_in, queries_ref), (span_in, span_ref), (store_in, store_ref))
+        )
+    ]
+    for copy in copies:
+        copy.start()
+    copies[0].wait()
     stack_heads(queries_ref, q_ref, rows)
+    copies[1].wait()
     attend(
         lambda index: lists_ref[me, index], lists_ref[me, lists_ref.shape[1] - 1], store_ref,
         span_ref, span_live_ref[0], q_ref, k_ref, v_ref, s_ref, ref_ref, acc_ref, rows, scale,
+        copies[2].wait,
     )
     finish(out_ref, ref_ref, acc_ref, rows, scale)
 
@@ -297,21 +332,11 @@
     )
 
 
-def project_kernel(peers, heads, me_ref, span_live_ref, *refs):
+def project_kernel(peers, heads, me_ref, turn_ref, span_live_ref, *refs):
     parts = refs[: 2 * peers - 1]
-    weight_ref, out_ref, held_ref, att_ref, sem_ref = refs[2 * peers - 1 :]
+    weight_ref, away_ref, keep_ref, att_ref, sorted_ref = refs[2 * peers - 1 :]
     rows, features = att_ref.shape
-    chunks, _, width = held_ref.shape
     head_dim = features // heads
-    copies = [
-        pltpu.make_async_copy(
-            weight_ref.at[:, pl.ds(i * width, width)], held_ref.at[i], sem_ref.at[i]
-        )
-        for i in range(chunks)
-    ]
-    for copy in copies:
-        copy.start()
-
     me = me_ref[0]
     logs = []
     for index, part in enumerate(parts):
@@ -335,29 +360,39 @@
             total += part[:rows, at].astype(jnp.float32) * weight[:, g : g + 1]
         att_ref[:, at] = total.astype(jnp.bfloat16)
 
-    for i in range(chunks):
-        copies[i].wait()
-        out_ref[:, i * width : (i + 1) * width] = jnp.dot(
-            att_ref[...], held_ref[i], preferred_element_type=jnp.float32
+    chips = keep_ref.shape[0]
+    block = keep_ref.shape[1]
+    chip, core = turn_ref[0] // 2, lax.rem(turn_ref[0], 2)
+    for side, wanted in enumerate((1 - core, core)):
+        for k in range(chips):
+            owner = 2 * lax.rem(chip + k, chips) + wanted
+            at = (side * chips + k) * block
+            sorted_ref[at : at + block, :] = att_ref[
+                pl.ds(pl.multiple_of(owner * block, block), block), :
+            ]
+    width = 512
+    for i in range(weight_ref.shape[1] // width):
+        at = slice(i * width, (i + 1) * width)
+        product = jnp.dot(
+            sorted_ref[...], weight_ref[:, at], preferred_element_type=jnp.float32
         ).astype(jnp.bfloat16)
-
-
-def project(me, span_live, parts, out_weight, peers, heads):
+        for k in range(chips):
+            away_ref[k, :, at] = product[k * block : (k + 1) * block]
+            keep_ref[k, :, at] = product[(chips + k) * block : (chips + k + 1) * block]
+
+
+def project(me, turn, span_live, parts, out_weight, peers, heads, members):
     features, outputs = out_weight.shape
     rows = parts[0].shape[0] - 16
-    width = 512
-    chunks = outputs // width
+    block_shape = jax.ShapeDtypeStruct((members // 2, rows // members, outputs), jnp.bfloat16)
     return pl.pallas_call(
         functools.partial(project_kernel, peers, heads),
-        out_shape=jax.ShapeDtypeStruct((rows, outputs), jnp.bfloat16),
-        in_specs=[SMEM, SMEM]
-        + [VMEM] * len(parts)
-        + [pl.BlockSpec(memory_space=pl.ANY)],
-        out_specs=VMEM,
+        out_shape=(block_shape, block_shape),
+        in_specs=[SMEM, SMEM, SMEM] + [VMEM] * (len(parts) + 1),
+        out_specs=(VMEM, VMEM),
         scratch_shapes=[
-            pltpu.VMEM((chunks, features, width), jnp.bfloat16),
             pltpu.VMEM((rows, features), jnp.bfloat16),
-            pltpu.SemaphoreType.DMA((chunks,)),
+            pltpu.VMEM((rows, features), jnp.bfloat16),
         ],
         compiler_params=pltpu.CompilerParams(vmem_limit_bytes=VMEM_LIMIT),
         cost_estimate=pl.CostEstimate(
@@ -366,7 +401,48 @@
             transcendentals=0,
         ),
         name="project",
-    )(me, span_live, *parts, out_weight)
+    )(me, turn, span_live, *parts, out_weight)
+
+
+def add_kernel(kept_ref, come_ref, *out_refs):
+    for k, out_ref in enumerate(out_refs):
+        out_ref[...] = (
+            kept_ref[k + 1].astype(jnp.float32) + come_ref[k + 1].astype(jnp.float32)
+        ).astype(jnp.bfloat16)
+
+
+def total_kernel(kept_ref, come_ref, *refs):
+    total = kept_ref[0].astype(jnp.float32) + come_ref[0].astype(jnp.float32)
+    for ref in refs[:-1]:
+        total += ref[...].astype(jnp.float32)
+    refs[-1][...] = total.astype(jnp.bfloat16)
+
+
+def scatter_sum(away, keep, members):
+    chips, block, outputs = keep.shape
+    shape = jax.ShapeDtypeStruct((block, outputs), jnp.bfloat16)
+    params = pltpu.CompilerParams(vmem_limit_bytes=VMEM_LIMIT)
+    come = lax.ppermute(away, "tp", [(i, i ^ 1) for i in range(members)])
+    sums = pl.pallas_call(
+        add_kernel,
+        out_shape=[shape] * (chips - 1),
+        in_specs=[VMEM, VMEM],
+        out_specs=[VMEM] * (chips - 1),
+        compiler_params=params,
+        name="add_cores",
+    )(keep, come)
+    arrived = [
+        lax.ppermute(each, "tp", [(i, (i + 2 * (k + 1)) % members) for i in range(members)])
+        for k, each in enumerate(sums)
+    ]
+    return pl.pallas_call(
+        total_kernel,
+        out_shape=shape,
+        in_specs=[VMEM] * (2 + len(arrived)),
+        out_specs=VMEM,
+        compiler_params=params,
+        name="add_chips",
+    )(keep, come, *arrived)
 
 
 def pack_kernel(span_live_ref, owners_ref, span_ref, out_ref, counts_ref):
@@ -423,9 +499,15 @@
     own = pl.pallas_call(
         functools.partial(own_kernel, scale),
         out_shape=part_shape,
-        in_specs=[SMEM, SMEM, SMEM, VMEM, VMEM, VMEM],
+        in_specs=[SMEM, SMEM, SMEM, HBM, HBM, HBM],
         out_specs=VMEM,
-        scratch_shapes=scratch,
+        scratch_shapes=[
+            pltpu.VMEM(queries.shape, jnp.bfloat16),
+            pltpu.VMEM(cache_store.shape, jnp.bfloat16),
+            pltpu.VMEM(span_cache.shape, jnp.bfloat16),
+            pltpu.SemaphoreType.DMA((3,)),
+            *scratch,
+        ],
         compiler_params=params,
         cost_estimate=attention_cost(rows, 8 * rows, head_dim, heads),
         name="own_attention",
@@ -456,8 +538,12 @@
         parts.append(shift(part_b, away))
         parts.append(shift(part_a, -away))
 
-    partial = project(me, span_lengths, parts, out_weight, peers, heads)
-    projected = lax.psum_scatter(partial, "tp", scatter_dimension=0, tiled=True)
+    members = lax.axis_size("tp")
+    turn = lax.axis_index("tp").reshape(1)
+    away, keep = project(
+        me, turn, span_lengths, parts, out_weight, peers, heads, members
+    )
+    projected = scatter_sum(away, keep, members)
 
     outgoing = pl.pallas_call(
         pack_kernel,

time: 278 us -> 281 us (1.011); the launches traced: 273 us -> 283 us
  starting transfers between devices: 74.5 us -> 112 us
  Pallas kernels: 134 us -> 106 us
  between operations: 15.6 us -> 2.21 us
  waiting for transfers between devices: 32.3 us -> 43.3 us
    ppermute x12, starting transfers between devices: 74.4 us -> 109 us  [shift(): return lax.ppermute(value, 'inst', pairs)]
    ppermute x12, waiting for transfers between devices: 14.3 us -> 40.6 us  [shift(): return lax.ppermute(value, 'inst', pairs)]
    pallas_call x3, Pallas kernels: 78 us -> 55.6 us  [shards(): pl.pallas_call(functools.partial(guest_kernel, scale, width, rows), out_s...]
    pallas_call x1, Pallas kernels: 45.3 us -> 24.7 us  [shards(): pl.pallas_call(functools.partial(own_kernel, scale), out_shape=part_shape...]
    reduce_scatter x1 -> x0, waiting for transfers between devices: 18 us -> none  [shards(): projected = lax.psum_scatter(partial, 'tp', scatter_dimension=0, tiled=True)]
    pallas_call x1, Pallas kernels: 0.69 us -> 17.6 us  [route(): pl.pallas_call(route_kernel, out_shape=(jax.ShapeDtypeStruct((peers, widt...]
    pallas_call x1, Pallas kernels: 8.97 us -> 5.88 us  [project(): pl.pallas_call(functools.partial(project_kernel, peers, heads), out_shape...]
    ppermute x0 -> x2, starting transfers between devices: none -> 2.82 us  [the longest x1 2.75 us: scatter_sum(): lax.ppermute(each, 'tp', [(i, (i + 2 * (k + 1)) % members) for i in range...]
  transfers between devices with their start and end apart: 13 -> 14, of which waited for: 3 -> 4; matrix products, arithmetic and copies ran while one was open for 0% -> 0% of each run, Pallas kernels for 45% -> 29%
where the time goes in v1:
time: 281 us; the launch traced here: 283 us
  starting transfers between devices  112 us (40%)
  Pallas kernels  106 us (38%)
  waiting for transfers between devices  43.3 us (15%)
  blocking collectives  11.6 us (4%)
  local copies, waits for them, and re-layouts  8.35 us (3%)
    ppermute x12, starting transfers between devices, shift(): return lax.ppermute(value, 'inst', pairs)  109 us
    pallas_call x3, Pallas kernels, shards(): pl.pallas_call(functools.partial(guest_kernel, scale, width, rows), out_s...  55.6 us
    ppermute x12, waiting for transfers between devices, shift(): return lax.ppermute(value, 'inst', pairs)  40.6 us
    pallas_call x1, Pallas kernels, shards(): pl.pallas_call(functools.partial(own_kernel, scale), out_shape=part_shape...  24.7 us
    pallas_call x1, Pallas kernels, route(): pl.pallas_call(route_kernel, out_shape=(jax.ShapeDtypeStruct((peers, widt...  17.6 us
    all_to_all x1, blocking collectives, shards(): lax.all_to_all(outgoing, 'inst', split_axis=1, concat_axis=1, tiled=True)  11.6 us
    unnamed x16, local copies, waits for them, and re-layouts  7.62 us
    pallas_call x1, Pallas kernels, project(): pl.pallas_call(functools.partial(project_kernel, peers, heads), out_shape...  5.88 us
  transfers between devices with their start and end apart: 14, of which 4 were waited for; matrix products, arithmetic and copies ran while one was open for 0% of the time, Pallas kernels for 29%

profile of v1, /device:TPU:4, one launch (start us, length us, event | category | flops | bytes accessed | tf_op | source)
XLA Modules:
  0.0 282.9 jit_solution(4326572314313850546)
XLA Ops:
  1.3 17.6 %route.1 = (s32[4,256]{1,0:T(4,128)}, bf16[272,1024]{1,0:T(8,128)(2,1)}) custom-call(s32[1]{0:T(128)S(6)} %copy.14.live_ref, s32[1,512]{1,0:T(1,128)} %bitcast.7, s32[1,512]{1,0:T(1,128)} %slots_in.1, bf16[256,1024]{1,0:T(8,128)(2,1)} %queries_in.1), custom_call_target="tpu_custom_call" | custom-call | tf_op jit(solution)/shard_map/route/pallas_call | solution.py:87
  18.9 3.5 %collective-permute-start = (bf16[272,1024]{1,0:T(8,128)(2,1)}, bf16[272,1024]{1,0:T(8,128)(2,1)S(1)}, u32[]{:S(2)}, u32[]{:S(2)}) collective-permute-start(bf16[272,1024]{1,0:T(8,128)(2,1)} %get-tuple-element.19), channel_id=1, source_target_pairs={{0,4},{4,8},{8,12},{1,5},{5,9},{9,13},{2,6},{6,10},{10,14},{3,7},{... | collective-permute-start | bytes 1671176 | tf_op jit(solution)/shard_map/ppermute | solution.py:493
  22.4 1.3 collective-permute-start.1
  24.4 0.0 copy-start.1
  24.4 1.0 copy-done.1
  25.4 0.9 copy-done.2
  26.3 1.6 copy-done.5
  27.9 0.7 copy-done.7
  28.6 24.7 %own_attention.1.after_ref.refs_0_ = bf16[272,1024]{1,0:T(8,128)(2,1)S(1)} custom-call(s32[1]{0:T(128)} %bitcast.me_ref, s32[1]{0:T(128)S(6)} %copy.15.span_live_ref, s32[4,256]{1,0:T(4,128)S(1)} %copy-done.7, bf16[256,1024]{1,0:T(8,128)(2,1)S(1)} %copy-done.1, bf16[2,256,16,128]{3,2,1,0:T(8,128)(2,1)S(1)} %copy-done.5, bf16[2,256,128]{2,1,0:T(8,128)(2,1)S(1)} %copy-done.2), custom_call_target="tpu_custom_call" | custom-call | flops 2147483648 | bytes 4194304 | tf_op jit(solution)/shard_map/own_attention/pallas_call | solution.py:499
  53.3 0.0 collective-permute-done.a_ref
  53.4 0.0 collective-permute-done.1.b_ref
  53.4 1.3 collective-permute-start.4
  54.7 1.3 collective-permute-start.5
  56.0 11.4 %guest_attention.3 = (bf16[272,1024]{1,0:T(8,128)(2,1)S(1)}, bf16[272,1024]{1,0:T(8,128)(2,1)}) custom-call(s32[1]{0:T(128)} %bitcast.me_ref, bf16[272,1024]{1,0:T(8,128)(2,1)S(1)} %collective-permute-done.a_ref, bf16[272,1024]{1,0:T(8,128)(2,1)S(1)} %collective-permute-done.1.b_ref, bf16[2,256,16,128]{3,2,1,0:T(8,128)(2,1)S(1)} %copy-done.5, ...), custom_call_target="tpu_custom_call" | custom-call | flops 2147483648 | bytes 4194304 | tf_op jit(solution)/shard_map/guest_attention/pallas_call | solution.py:522
  67.4 0.0 collective-permute-done.4.a_ref
  67.4 26.7 %collective-permute-done.5.b_ref = bf16[272,1024]{1,0:T(8,128)(2,1)S(1)} collective-permute-done((bf16[272,1024]{1,0:T(8,128)(2,1)S(1)}, bf16[272,1024]{1,0:T(8,128)(2,1)S(1)}, u32[]{:S(2)}, u32[]{:S(2)}) %collective-permute-start.5) | collective-permute-done | bytes 557088 | tf_op jit(solution)/shard_map/ppermute | solution.py:493
  94.1 74.1 %collective-permute-start.8 = (bf16[272,1024]{1,0:T(8,128)(2,1)S(1)}, bf16[272,1024]{1,0:T(8,128)(2,1)S(1)}, u32[]{:S(2)}, u32[]{:S(2)}) collective-permute-start(bf16[272,1024]{1,0:T(8,128)(2,1)S(1)} %collective-permute-done.4.a_ref), channel_id=1, source_target_pairs={{0,4},{4,8},{8,12},{1,5},{5,9},{9,13},{2,6},{6,10},{10,14},{3,7},{... | collective-permute-start | bytes 1671176 | tf_op jit(solution)/shard_map/ppermute | solution.py:493
  168.2 1.3 collective-permute-start.9
  169.5 1.3 collective-permute-start.3
  170.8 5.2 %collective-permute-start.2 = (bf16[272,1024]{1,0:T(8,128)(2,1)}, bf16[272,1024]{1,0:T(8,128)(2,1)S(1)}, u32[]{:S(2)}, u32[]{:S(2)}) collective-permute-start(bf16[272,1024]{1,0:T(8,128)(2,1)} %get-tuple-element.21), channel_id=1, source_target_pairs={{0,4},{4,8},{8,12},{1,5},{5,9},{9,13},{2,6},{6,10},{10,14},{3,7},{... | collective-permute-start | bytes 1671176 | tf_op jit(solution)/shard_map/ppermute | solution.py:493
  176.0 0.0 copy-done.6
  176.0 32.6 %guest_attention.4 = (bf16[272,1024]{1,0:T(8,128)(2,1)}, bf16[272,1024]{1,0:T(8,128)(2,1)}) custom-call(s32[1]{0:T(128)} %bitcast.me_ref, bf16[272,1024]{1,0:T(8,128)(2,1)S(1)} %collective-permute-done.4.a_ref, bf16[272,1024]{1,0:T(8,128)(2,1)S(1)} %collective-permute-done.5.b_ref, bf16[2,256,16,128]{3,2,1,0:T(8,128)(2,1)S(1)} %copy-done.6, ...), custom_call_target="tpu_custom_call" | custom-call | flops 2147483648 | bytes 4194304 | tf_op jit(solution)/shard_map/guest_attention/pallas_call | solution.py:522
  208.6 15.9 %collective-permute-start.6 = (bf16[272,1024]{1,0:T(8,128)(2,1)}, bf16[272,1024]{1,0:T(8,128)(2,1)S(1)}, u32[]{:S(2)}, u32[]{:S(2)}) collective-permute-start(bf16[272,1024]{1,0:T(8,128)(2,1)} %get-tuple-element.26), channel_id=1, source_target_pairs={{0,8},{4,12},{1,9},{5,13},{2,10},{6,14},{3,11},{7,15},{16,24},{20,... | collective-permute-start | bytes 1671176 | tf_op jit(solution)/shard_map/ppermute | solution.py:493
  224.5 0.0 collective-permute-done.8.a_ref
  224.6 1.3 collective-permute-start.7
  225.9 0.0 collective-permute-done.9.b_ref
  225.9 0.0 copy-start.3
  225.9 11.6 %guest_attention.5 = (bf16[272,1024]{1,0:T(8,128)(2,1)}, bf16[272,1024]{1,0:T(8,128)(2,1)}) custom-call(s32[1]{0:T(128)} %bitcast.me_ref, bf16[272,1024]{1,0:T(8,128)(2,1)S(1)} %collective-permute-done.8.a_ref, bf16[272,1024]{1,0:T(8,128)(2,1)S(1)} %collective-permute-done.9.b_ref, bf16[2,256,16,128]{3,2,1,0:T(8,128)(2,1)S(1)} %copy-done.6, ...), custom_call_target="tpu_custom_call" | custom-call | flops 2147483648 | bytes 4194304 | tf_op jit(solution)/shard_map/guest_attention/pallas_call | solution.py:522
  237.5 0.0 copy-start.4
  237.5 1.3 collective-permute-start.10
  238.8 0.0 collective-permute-done.3.refs_2_
  238.8 1.3 collective-permute-start.11
  240.1 0.0 collective-permute-done.2.refs_1_
  240.1 0.0 collective-permute-done.6.refs_3_
  240.1 0.0 collective-permute-done.7.refs_4_
  240.2 7.9 %collective-permute-done.10.refs_5_ = bf16[272,1024]{1,0:T(8,128)(2,1)S(1)} collective-permute-done((bf16[272,1024]{1,0:T(8,128)(2,1)}, bf16[272,1024]{1,0:T(8,128)(2,1)S(1)}, u32[]{:S(2)}, u32[]{:S(2)}) %collective-permute-start.10) | collective-permute-done | bytes 557088 | tf_op jit(solution)/shard_map/ppermute | solution.py:493
  248.1 6.0 %collective-permute-done.11.refs_6_ = bf16[272,1024]{1,0:T(8,128)(2,1)} collective-permute-done((bf16[272,1024]{1,0:T(8,128)(2,1)}, bf16[272,1024]{1,0:T(8,128)(2,1)}, u32[]{:S(2)}, u32[]{:S(2)}) %collective-permute-start.11) | collective-permute-done | bytes 557088 | tf_op jit(solution)/shard_map/ppermute | solution.py:493
  254.1 3.4 %copy-done = bf16[1024,4096]{1,0:T(8,128)(2,1)S(1)} copy-done((bf16[1024,4096]{1,0:T(8,128)(2,1)S(1)}, bf16[1024,4096]{1,0:T(8,128)(2,1)}, u32[]{:S(2)}) %copy-start) | copy-done | bytes 8388632
  257.4 5.9 %project.1 = (bf16[2,64,4096]{2,1,0:T(8,128)(2,1)S(1)}, bf16[2,64,4096]{2,1,0:T(8,128)(2,1)S(1)}) custom-call(s32[1]{0:T(128)} %bitcast.me_ref, s32[1]{0:T(128)} %bitcast.1.turn_ref, s32[1]{0:T(128)S(6)} %copy.15.span_live_ref, bf16[272,1024]{1,0:T(8,128)(2,1)S(1)} %own_attention.1.after_ref.refs_0_, bf16[272,1024]{1,0:T(8,128)(2,1)S(1)} %collective-permute-done.2.refs_1_, ...), custom_call_target="tpu_custom_call" | custom-call | flops 2147483648 | bytes 10485760 | tf_op jit(solution)/shard_map/project/pallas_call | solution.py:388
  263.3 0.1 collective-permute-start.12
  263.4 2.6 collective-permute-done.12.come_ref
  266.0 0.1 add_cores.1
  266.2 2.7 collective-permute-start.13
  268.9 0.6 pack_blocks.1
  269.6 11.6 %all_to_all.5 = bf16[2,4,8,16,128]{4,3,2,0,1:T(8,128)(2,1)S(1)} all-to-all(bf16[2,4,8,16,128]{4,3,2,0,1:T(8,128)(2,1)S(1)} %copy.12), channel_id=1, replica_groups=mesh['pods'=2,'inst'=4,'tp'=4] {'inst'}, dimensions={1} | all-to-all | bytes 524288 | tf_op jit(solution)/shard_map/all_to_all | solution.py:559
  281.1 0.7 copy.13
  281.9 0.0 collective-permute-done.13.refs_0_
  281.9 1.0 add_chips.1
  (8 shorter events, 0.0 us)
Async XLA Ops:
  18.9 34.5 %collective-permute-start = (bf16[272,1024]{1,0:T(8,128)(2,1)}, bf16[272,1024]{1,0:T(8,128)(2,1)S(1)}, u32[]{:S(2)}, u32[]{:S(2)}) collective-permute-start(bf16[272,1024]{1,0:T(8,128)(2,1)} %get-tuple-element.19), channel_id=1, source_target_pairs={{0,4},{4,8},{8,12},{1,5},{5,9},{9,13},{2,6},{6,10},{10,14},{3,7},{... | collective-permute-start | bytes 1671176 | tf_op jit(solution)/shard_map/ppermute | solution.py:493
  22.4 30.9 %collective-permute-start.1 = (bf16[272,1024]{1,0:T(8,128)(2,1)}, bf16[272,1024]{1,0:T(8,128)(2,1)S(1)}, u32[]{:S(2)}, u32[]{:S(2)}) collective-permute-start(bf16[272,1024]{1,0:T(8,128)(2,1)} %get-tuple-element.19), channel_id=1, source_target_pairs={{4,0},{8,4},{12,8},{5,1},{9,5},{13,9},{6,2},{10,6},{14,10},{7,3},{... | collective-permute-start | bytes 1671176 | tf_op jit(solution)/shard_map/ppermute | solution.py:493
  24.4 1.0 copy-start.1
  25.4 0.9 copy-start.2
  26.3 1.6 copy-start.5
  27.9 0.7 copy-start.7
  28.6 147.4 %copy-start.6 = (bf16[2,256,16,128]{3,2,1,0:T(8,128)(2,1)S(1)}, bf16[2,256,16,128]{3,2,1,0:T(8,128)(2,1)}, u32[]{:S(2)}) copy-start(bf16[2,256,16,128]{3,2,1,0:T(8,128)(2,1)} %store_ref.5) | copy-start | bytes 6291460
  53.4 14.0 %collective-permute-start.4 = (bf16[272,1024]{1,0:T(8,128)(2,1)S(1)}, bf16[272,1024]{1,0:T(8,128)(2,1)S(1)}, u32[]{:S(2)}, u32[]{:S(2)}) collective-permute-start(bf16[272,1024]{1,0:T(8,128)(2,1)S(1)} %collective-permute-done.a_ref), channel_id=1, source_target_pairs={{0,4},{4,8},{8,12},{1,5},{5,9},{9,13},{2,6},{6,10},{10,14},{3,7},{... | collective-permute-start | bytes 1671176 | tf_op jit(solution)/shard_map/ppermute | solution.py:493
  54.7 39.4 %collective-permute-start.5 = (bf16[272,1024]{1,0:T(8,128)(2,1)S(1)}, bf16[272,1024]{1,0:T(8,128)(2,1)S(1)}, u32[]{:S(2)}, u32[]{:S(2)}) collective-permute-start(bf16[272,1024]{1,0:T(8,128)(2,1)S(1)} %collective-permute-done.1.b_ref), channel_id=1, source_target_pairs={{4,0},{8,4},{12,8},{5,1},{9,5},{13,9},{6,2},{10,6},{14,10},{7,3},{... | collective-permute-start | bytes 1671176 | tf_op jit(solution)/shard_map/ppermute | solution.py:493
  94.1 130.4 %collective-permute-start.8 = (bf16[272,1024]{1,0:T(8,128)(2,1)S(1)}, bf16[272,1024]{1,0:T(8,128)(2,1)S(1)}, u32[]{:S(2)}, u32[]{:S(2)}) collective-permute-start(bf16[272,1024]{1,0:T(8,128)(2,1)S(1)} %collective-permute-done.4.a_ref), channel_id=1, source_target_pairs={{0,4},{4,8},{8,12},{1,5},{5,9},{9,13},{2,6},{6,10},{10,14},{3,7},{... | collective-permute-start | bytes 1671176 | tf_op jit(solution)/shard_map/ppermute | solution.py:493
  168.2 57.7 %collective-permute-start.9 = (bf16[272,1024]{1,0:T(8,128)(2,1)S(1)}, bf16[272,1024]{1,0:T(8,128)(2,1)S(1)}, u32[]{:S(2)}, u32[]{:S(2)}) collective-permute-start(bf16[272,1024]{1,0:T(8,128)(2,1)S(1)} %collective-permute-done.5.b_ref), channel_id=1, source_target_pairs={{4,0},{8,4},{12,8},{5,1},{9,5},{13,9},{6,2},{10,6},{14,10},{7,3},{... | collective-permute-start | bytes 1671176 | tf_op jit(solution)/shard_map/ppermute | solution.py:493
  169.5 69.4 %collective-permute-start.3 = (bf16[272,1024]{1,0:T(8,128)(2,1)S(1)}, bf16[272,1024]{1,0:T(8,128)(2,1)S(1)}, u32[]{:S(2)}, u32[]{:S(2)}) collective-permute-start(bf16[272,1024]{1,0:T(8,128)(2,1)S(1)} %get-tuple-element.25.after_ref), channel_id=1, source_target_pairs={{4,0},{8,4},{12,8},{5,1},{9,5},{13,9},{6,2},{10,6},{14,10},{7,3},{... | collective-permute-start | bytes 1671176 | tf_op jit(solution)/shard_map/ppermute | solution.py:493
  170.8 69.4 %collective-permute-start.2 = (bf16[272,1024]{1,0:T(8,128)(2,1)}, bf16[272,1024]{1,0:T(8,128)(2,1)S(1)}, u32[]{:S(2)}, u32[]{:S(2)}) collective-permute-start(bf16[272,1024]{1,0:T(8,128)(2,1)} %get-tuple-element.21), channel_id=1, source_target_pairs={{0,4},{4,8},{8,12},{1,5},{5,9},{9,13},{2,6},{6,10},{10,14},{3,7},{... | collective-permute-start | bytes 1671176 | tf_op jit(solution)/shard_map/ppermute | solution.py:493
  208.6 31.5 %collective-permute-start.6 = (bf16[272,1024]{1,0:T(8,128)(2,1)}, bf16[272,1024]{1,0:T(8,128)(2,1)S(1)}, u32[]{:S(2)}, u32[]{:S(2)}) collective-permute-start(bf16[272,1024]{1,0:T(8,128)(2,1)} %get-tuple-element.26), channel_id=1, source_target_pairs={{0,8},{4,12},{1,9},{5,13},{2,10},{6,14},{3,11},{7,15},{16,24},{20,... | collective-permute-start | bytes 1671176 | tf_op jit(solution)/shard_map/ppermute | solution.py:493
  224.6 15.6 %collective-permute-start.7 = (bf16[272,1024]{1,0:T(8,128)(2,1)}, bf16[272,1024]{1,0:T(8,128)(2,1)S(1)}, u32[]{:S(2)}, u32[]{:S(2)}) collective-permute-start(bf16[272,1024]{1,0:T(8,128)(2,1)} %get-tuple-element.27.after_ref), channel_id=1, source_target_pairs={{8,0},{12,4},{9,1},{13,5},{10,2},{14,6},{11,3},{15,7},{24,16},{28,... | collective-permute-start | bytes 1671176 | tf_op jit(solution)/shard_map/ppermute | solution.py:493
  225.9 43.1 %copy-start.3 = (bf16[2,256,128]{2,1,0:T(8,128)(2,1)S(1)}, bf16[2,256,128]{2,1,0:T(8,128)(2,1)}, u32[]{:S(2)}) copy-start(bf16[2,256,128]{2,1,0:T(8,128)(2,1)} %span_ref.1) | copy-start | bytes 393220
  237.5 31.5 %copy-start.4 = (s32[1,16,1]{1,2,0:T(1,128)S(1)}, s32[1,16,1]{1,2,0:T(1,128)}, u32[]{:S(2)}) copy-start(s32[1,16,1]{1,2,0:T(1,128)} %param.17) | copy-start | bytes 196
  237.5 10.6 %collective-permute-start.10 = (bf16[272,1024]{1,0:T(8,128)(2,1)}, bf16[272,1024]{1,0:T(8,128)(2,1)S(1)}, u32[]{:S(2)}, u32[]{:S(2)}) collective-permute-start(bf16[272,1024]{1,0:T(8,128)(2,1)} %get-tuple-element.30), channel_id=1, source_target_pairs={{0,12},{1,13},{2,14},{3,15},{16,28},{17,29},{18,30},{19,31}} | collective-permute-start | bytes 1671176 | tf_op jit(solution)/shard_map/ppermute | solution.py:493
  238.8 15.2 %collective-permute-start.11 = (bf16[272,1024]{1,0:T(8,128)(2,1)}, bf16[272,1024]{1,0:T(8,128)(2,1)}, u32[]{:S(2)}, u32[]{:S(2)}) collective-permute-start(bf16[272,1024]{1,0:T(8,128)(2,1)} %get-tuple-element.31), channel_id=1, source_target_pairs={{12,0},{13,1},{14,2},{15,3},{28,16},{29,17},{30,18},{31,19}} | collective-permute-start | bytes 1671176 | tf_op jit(solution)/shard_map/ppermute | solution.py:493
  254.1 3.4 %copy-start = (bf16[1024,4096]{1,0:T(8,128)(2,1)S(1)}, bf16[1024,4096]{1,0:T(8,128)(2,1)}, u32[]{:S(2)}) copy-start(bf16[1024,4096]{1,0:T(8,128)(2,1)} %refs_7_.1) | copy-start | bytes 25165828
  263.3 2.7 collective-permute-start.12
  266.2 15.7 %collective-permute-start.13 = (bf16[64,4096]{1,0:T(8,128)(2,1)S(1)}, bf16[64,4096]{1,0:T(8,128)(2,1)S(1)}, u32[]{:S(2)}, u32[]{:S(2)}) collective-permute-start(bf16[64,4096]{1,0:T(8,128)(2,1)S(1)} %add_cores.1), channel_id=1, source_target_pairs={{0,2},{1,3},{2,0},{3,1},{4,6},{5,7},{6,4},{7,5},{8,10},{9,11},{10,... | collective-permute-start | bytes 1572872 | tf_op jit(solution)/shard_map/ppermute | solution.py:435
